TPU v7x, 512 devices: a whole 4x4x16 slice. The times are simulated.
512 devices in a mesh: rep: 4 (over y_hi, core), fsdp: 32 (over z, y_lo), tp: 4 (over x).
Axes of the slice: x: 4, y: 4 (y_hi: 2, y_lo: 2; y = y_hi * 2 + y_lo), z: 16, core: 2. Of those that a mesh axis runs over, the one named last changes fastest.
Arguments:
- master: float32 [128, 32, 14336], P(('rep', 'fsdp'), 'tp'), may hold values from -0.06 to 0.06
- moment_one: float32 [128, 32, 14336], P(('rep', 'fsdp'), 'tp'), may hold values from -2 to 2
- moment_two: float32 [128, 32, 14336], P(('rep', 'fsdp'), 'tp'), may hold values from 0.001 to 0.01
- grads: bfloat16 [4, 4, 32, 32, 14336], P('rep', None, 'fsdp', 'tp'), may hold values from -6 to 6
- inputs: bfloat16 [1024, 4096], P('fsdp'), may hold values from -6 to 6
- out_grad: bfloat16 [1024, 14336], P('fsdp', 'tp'), may hold values from -6 to 6
Outputs:
- new_master: float32 [128, 32, 14336], P(('rep', 'fsdp'), 'tp')
- new_one: float32 [128, 32, 14336], P(('rep', 'fsdp'), 'tp')
- new_two: float32 [128, 32, 14336], P(('rep', 'fsdp'), 'tp')
- forward_part: bfloat16 [4, 4, 1024, 14336], P('rep', 'tp', 'fsdp')
- backward_part: bfloat16 [4, 1024, 4096], P('tp', 'fsdp', 'rep')
All inputs are finite; a program needn't handle non-finite values.
Results may differ from a plain program's by a relative error of at most 0.019.
Values may be sent and summed in bfloat16 or wider, within the bound.
A program may use at most 128 MiB of HBM per device.

v0:
```python
import jax
import jax.numpy as jnp
from jax import lax
from jax.sharding import PartitionSpec as P

beta_one = 0.9
beta_two = 0.95
learn_rate = 0.003
decay_rate = 0.1
block_width = 32


def unit_clip(values):
    lead, rows_here, width = values.shape
    blocks = values.reshape(lead, rows_here, width // block_width, block_width)
    unit_level = 2.5 * jnp.mean(jnp.abs(blocks), axis=3, keepdims=True)
    return (
        jnp.clip(blocks, -unit_level, unit_level)
        .reshape(lead, rows_here, width)
        .astype(jnp.bfloat16)
    )


def local(master, moment_one, moment_two, grads, inputs, out_grad):
    rep_count = lax.axis_size("rep")
    fsdp_count = lax.axis_size("fsdp")
    tp_count = lax.axis_size("tp")
    summed = lax.psum_scatter(
        grads.astype(jnp.float32).astype(jnp.bfloat16), "rep", scatter_dimension=1, tiled=True
    ).astype(jnp.float32)
    grad = summed.reshape(master.shape) / rep_count
    new_one = beta_one * moment_one + (1.0 - beta_one) * grad
    new_two = beta_two * moment_two + (1.0 - beta_two) * grad * grad
    fix_one = 1.0 - beta_one**10
    fix_two = 1.0 - beta_two**10
    step_dir = new_one / fix_one / (jnp.sqrt(new_two / fix_two) + 1e-08)
    new_master = master - learn_rate * (step_dir + decay_rate * master)
    local_rows = master.shape[1]
    hidden = master.shape[2]
    band_rows = local_rows * tp_count
    partial_sums = jnp.sum(jnp.abs(new_master), axis=1, keepdims=True)
    total = lax.psum(partial_sums.astype(jnp.bfloat16), "tp").astype(jnp.float32)
    band_level = 2.5 * (total / band_rows)
    band_copy = jnp.clip(new_master, -band_level, band_level).astype(jnp.bfloat16)
    tiles = lax.all_to_all(
        new_master.astype(jnp.bfloat16), "tp", split_axis=2, concat_axis=1, tiled=True
    ).astype(new_master.dtype)
    unit_copy = unit_clip(tiles)
    tokens_here = inputs.shape[0]
    rep_index = lax.axis_index("rep")
    tp_index = lax.axis_index("tp")
    x_view = inputs.reshape(tokens_here, rep_count, fsdp_count, tp_count, local_rows)
    chosen = lax.dynamic_index_in_dim(x_view, rep_index, 1, keepdims=False)
    chosen = lax.dynamic_index_in_dim(chosen, tp_index, 2, keepdims=False)
    piece = lax.all_gather(band_copy, "fsdp", axis=0, tiled=True)
    count = piece.shape[0]
    left = chosen.reshape(tokens_here, count * local_rows)
    forward = jnp.dot(
        left, piece.reshape(count * local_rows, hidden), preferred_element_type=jnp.float32
    )
    piece = lax.all_gather(unit_copy, "fsdp", axis=0, tiled=True)
    flat = piece.reshape(piece.shape[0] * piece.shape[1], piece.shape[2])
    backward = lax.dot_general(
        out_grad, flat, (((1,), (1,)), ((), ())), preferred_element_type=jnp.float32
    )
    forward_part = forward.astype(jnp.bfloat16).reshape(1, 1, tokens_here, hidden)
    backward_part = backward.astype(jnp.bfloat16).reshape(1, tokens_here, fsdp_count * band_rows)
    return (new_master, new_one, new_two, forward_part, backward_part)


def solution(mesh):
    placed = (
        P(("rep", "fsdp"), "tp", None),
        P(("rep", "fsdp"), "tp", None),
        P(("rep", "fsdp"), "tp", None),
        P("rep", None, "fsdp", "tp", None),
        P("fsdp", None),
        P("fsdp", "tp"),
    )
    return jax.shard_map(
        local,
        mesh=mesh,
        in_specs=placed,
        out_specs=(
            P(("rep", "fsdp"), "tp", None),
            P(("rep", "fsdp"), "tp", None),
            P(("rep", "fsdp"), "tp", None),
            P("rep", "tp", "fsdp", None),
            P("tp", "fsdp", "rep"),
        ),
        check_vma=False,
    )
```

profile of v0, /device:TPU:6, one launch (start us, length us, event | category | flops | bytes accessed | tf_op | source)
XLA Modules:
  0.0 445.0 jit_solution(9177928997389883990)
XLA Ops:
  7.2 0.0 reduce-scatter.2.cloned.1.call-start
  7.2 0.7 reduce-scatter.2.cloned.1.call-update
  7.9 0.0 all-gather.3.cloned.1.call-start
  8.0 54.1 %reduce-scatter.2.cloned.1.call-done = bf16[1,1,1,8,14336]{4,3,2,1,0:T(8,128)(2,1)} async-done(((bf16[1,4,1,8,14336]{4,3,2,1,0:T(8,128)(2,1)}), bf16[1,1,1,8,14336]{4,3,2,1,0:T(8,128)(2,1)}) %reduce-scatter.2.cloned.1.call-update) | async-done | bytes 229392 | tf_op jit(solution)/shard_map/reduce_scatter | solution.py:28
  62.0 2.7 fusion.15
  64.7 0.2 abs_reduce_fusion
  64.9 14.6 %psum.7 = bf16[1,1,14336]{2,1,0:T(2,128)(2,1)S(1)} all-reduce(bf16[1,1,14336]{2,1,0:T(2,128)(2,1)S(1)} %convert_element_type.90), channel_id=1, replica_groups=mesh['rep'=4,'fsdp'=32,'tp'=4] {'tp'}, use_global_device_ids=true, to_apply=%region_2.0 | all-reduce | flops 14336 | bytes 57344 | tf_op jit(solution)/shard_map/psum | solution.py:42
  79.5 0.1 convert_multiply_fusion.3
  79.6 0.8 minimum_convert_fusion
  80.4 0.0 all-gather.5.cloned.1.call-start
  80.4 11.5 %copy.13 = bf16[1,8,14336]{1,0,2:T(2,128)(2,1)} copy(bf16[1,8,14336]{2,1,0:T(8,128)(2,1)S(1)} %get-tuple-element.5) | data formatting | bytes 458752 | tf_op jit(solution)/shard_map/convert_element_type | solution.py:46
  91.9 0.5 broadcast.63
  92.4 79.7 %reduce.3 = bf16[14336,8]{1,0:T(8,128)(2,1)} reduce(bf16[14336,1,8]{2,1,0:T(2,128)(2,1)} %bitcast.47, bf16[]{:T(256)} %broadcast.63), dimensions={1}, to_apply=%bitcast.37.reduce_sub_computation | reduce | bytes 458754
  172.2 5.2 %reshape.192 = bf16[4,2,14336]{2,1,0:T(2,128)(2,1)S(1)} reshape(bf16[14336,8]{1,0:T(8,128)(2,1)} %reduce.3) | data formatting | bytes 458752
  177.4 10.4 %all_to_all.4 = bf16[4,2,14336]{2,1,0:T(2,128)(2,1)S(1)} all-to-all(bf16[4,2,14336]{2,1,0:T(2,128)(2,1)S(1)} %reshape.192), channel_id=1, replica_groups=mesh['rep'=4,'fsdp'=32,'tp'=4] {'tp'}, dimensions={0} | all-to-all | bytes 458752 | tf_op jit(solution)/shard_map/all_to_all | solution.py:45
  187.8 9.6 %reshape.193 = bf16[14336,1,8]{2,1,0:T(2,128)(2,1)} reshape(bf16[4,2,14336]{2,1,0:T(2,128)(2,1)S(1)} %all_to_all.4) | data formatting | bytes 458752
  197.4 12.2 %convert_abs_fusion = f32[1,8,14336]{1,0,2:T(1,128)} fusion(bf16[14336,1,8]{2,1,0:T(2,128)(2,1)} %reshape.193), kind=kLoop, calls=%fused_computation.24 | loop fusion | flops 229376 | bytes 688128 | tf_op jit(solution)/shard_map/abs | solution.py:16
  209.7 4.9 %copy.14 = f32[1,8,4,3584]{3,1,2,0:T(8,128)S(1)} copy(f32[1,8,4,3584]{1,3,2,0:T(8,128)} %bitcast.46) | data formatting | bytes 917504 | tf_op jit(solution)/shard_map/abs | solution.py:16
  214.5 0.5 abs.30
  215.1 0.6 reduce_sum.19
  215.7 0.5 min.41
  216.2 0.9 min.42
  217.1 0.5 max.41
  217.6 0.9 max.42
  218.5 9.7 %bitcast_convert_fusion = f32[1,8,14336]{1,0,2:T(1,128)} fusion(bf16[14336,1,8]{2,1,0:T(2,128)(2,1)} %reshape.193), kind=kLoop, calls=%fused_computation.28 | loop fusion | flops 114688 | bytes 688128 | tf_op jit(solution)/shard_map/convert_element_type | solution.py:47
  228.3 4.3 copy.15
  232.6 0.7 fusion.9
  233.4 0.5 copy.12
  233.9 22.4 %all-gather.3.cloned.1.call-done = bf16[32,8,14336]{2,1,0:T(8,128)(2,1)} async-done(((bf16[1,8,14336]{2,1,0:T(8,128)(2,1)}), bf16[32,8,14336]{2,1,0:T(8,128)(2,1)}) %all-gather.3.cloned.1.call-update) | async-done | bytes 7340048 | tf_op jit(solution)/shard_map/all_gather | solution.py:55
  256.3 5.4 %fusion = bf16[1,1,32,14336]{3,2,1,0:T(8,128)(2,1)} fusion(bf16[32,8,14336]{2,1,0:T(8,128)(2,1)} %all-gather.3.cloned.1.call-done, bf16[32,4,32,4,8]{0,4,3,2,1:T(8,128)(2,1)S(1)} %bitcast.50, s32[]{:T(128)S(6)} %select_n.13, s32[]{:T(128)S(6)} %select_n.15), kind=kOutput, calls=%fused_computation.1 | convolution fusion | flops 235339776 | bytes 8323080 | tf_op jit(solution)/shard_map/dot_general | solution.py:58
  261.7 170.8 %all-gather.5.cloned.1.call-done = bf16[32,32,3584]{2,1,0:T(8,128)(2,1)} async-done(((bf16[1,32,3584]{2,1,0:T(8,128)(2,1)}), bf16[32,32,3584]{2,1,0:T(8,128)(2,1)}) %all-gather.5.cloned.1.call-update) | async-done | bytes 7340048 | tf_op jit(solution)/shard_map/all_gather | solution.py:61
  432.5 5.9 %fusion.2 = bf16[1,32,1024]{2,1,0:T(8,128)(2,1)} fusion(bf16[1024,3584]{1,0:T(8,128)(2,1)} %bitcast.48, bf16[32,3584]{1,0:T(8,128)(2,1)S(1)} %copy-done), kind=kOutput, calls=%fused_computation.4 | convolution fusion | flops 234913792 | bytes 7634944 | tf_op jit(solution)/shard_map/dot_general | solution.py:63
  (10 shorter events, 0.1 us)
Async XLA Ops:
  7.2 425.4 %copy-start = (bf16[32,3584]{1,0:T(8,128)(2,1)S(1)}, bf16[32,3584]{1,0:T(8,128)(2,1)}, u32[]{:S(2)}) copy-start(bf16[32,3584]{1,0:T(8,128)(2,1)} %param.11) | copy-start | bytes 688132
  7.2 54.8 %reduce-scatter.2.cloned.1.call-start = ((), (), s32[]{:S(2)}) async-start(), calls=%async_computation.2 | async-start | bytes 1146880 | tf_op jit(solution)/shard_map/reduce_scatter | solution.py:28
  7.9 248.3 %all-gather.3.cloned.1.call-start = ((), (), s32[]{:S(2)}) async-start(), calls=%async_computation.3 | async-start | bytes 7569408 | tf_op jit(solution)/shard_map/all_gather | solution.py:55
  64.7 107.4 %copy-start.1 = (f32[1,8,14336]{2,1,0:T(8,128)}, f32[1,8,14336]{2,1,0:T(8,128)S(1)}, u32[]{:S(2)}) copy-start(f32[1,8,14336]{2,1,0:T(8,128)S(1)} %get-tuple-element.6) | copy-start | bytes 1376260
  80.4 352.1 %all-gather.5.cloned.1.call-start = ((), (), s32[]{:S(2)}) async-start(), calls=%async_computation.4 | async-start | bytes 7569408 | tf_op jit(solution)/shard_map/all_gather | solution.py:61
  228.2 5.1 %copy-start.2 = (bf16[32,4096]{1,0:T(8,128)(2,1)S(1)}, bf16[32,4096]{1,0:T(8,128)(2,1)}, u32[]{:S(2)}) copy-start(bf16[32,4096]{1,0:T(8,128)(2,1)} %param.10) | copy-start | bytes 786436
Sparse Core Ops, SparseCore 0:
  11.1 50.8 reduce-scatter.1
  80.5 175.7 all-gather.2
  258.5 173.9 all-gather.4
where the time goes:
time: 445 us
  waiting for transfers between devices  248 us (56%)
  other arithmetic  107 us (24%)
  local copies, waits for them, and re-layouts  39.9 us (9%)
  blocking collectives  25 us (6%)
  between operations  13.9 us (3%)
  matrix products  11.4 us (3%)
    all_gather x1, waiting for transfers between devices, local(): piece = lax.all_gather(unit_copy, 'fsdp', axis=0, tiled=True)  171 us
    unnamed x1, other arithmetic  79.7 us
    reduce_scatter x1, waiting for transfers between devices, local(): lax.psum_scatter(grads.astype(jnp.float32).astype(jnp.bfloat16), 'rep', s...  54.1 us
    all_gather x1, waiting for transfers between devices, local(): piece = lax.all_gather(band_copy, 'fsdp', axis=0, tiled=True)  22.4 us
    unnamed x10, local copies, waits for them, and re-layouts  15.8 us
    psum x1, blocking collectives, local(): lax.psum(partial_sums.astype(jnp.bfloat16), 'tp').astype(jnp.float32)  14.6 us
    abs x1, other arithmetic, unit_clip(): unit_level = 2.5 * jnp.mean(jnp.abs(blocks), axis=3, keepdims=True)  12.2 us
    convert_element_type x1, local copies, waits for them, and re-layouts, local(): new_master.astype(jnp.bfloat16)  11.5 us
  transfers between devices with their start and end apart: 3, of which 3 were waited for; matrix products, arithmetic and copies ran while one was open for 33% of the time, Pallas kernels for 0%

commit v1 on v0

v1 whole, which is shorter than its diff:
```python
import functools

import jax
import jax.numpy as jnp
from jax import lax
from jax.experimental import pallas as pl
from jax.experimental.pallas import tpu as pltpu
from jax.sharding import PartitionSpec as P

beta_one = 0.9
beta_two = 0.95
learn_rate = 0.003
decay_rate = 0.1
block_width = 32

MESH = pl.DeviceIdType.MESH
F32 = jnp.float32
BF16 = jnp.bfloat16

UNIT = 1024
MSG = UNIT + 128
LEAD = 3


def kernel(
    nz, nu,
    master, mone, mtwo, grads, inputs, ograd,
    o_master, o_one, o_two, o_fwd, o_bwd,
    m0, m1, m2, gr, xa, xs, ogb, sel, ones,
    sa, ra, keep, sb, rb, ys, yr, ps, pr, g, fo, acc, bs, br, bo,
    ld, sa_s, sa_r, sb_s, sb_r, ys_s, ys_r, ps_s, ps_r, ring_s, ring_r,
    og_s, og_r, sh_s, sh_r, xs_s, xs_r, fo_s, fo_r, fo_l, bw_s, bw_r, out_s,
):
    half = nu * UNIT
    rep = lax.axis_index("rep")
    fs = lax.axis_index("fsdp")
    t = lax.axis_index("tp")
    nf = 2 * nz
    yh = lax.div(rep, 2)
    k = lax.rem(rep, 2)
    z = lax.div(fs, 2)
    y = lax.rem(fs, 2)
    first_core = k == 0
    first_y = y == 0

    sibling = {"rep": rep + 1 - 2 * k}
    opposite = {"rep": lax.rem(rep + 2, 4)}
    up = {"fsdp": lax.rem(fs + 2, nf)}
    down = {"fsdp": lax.rem(fs + nf - 2, nf)}
    mate = {"fsdp": fs + 1 - 2 * y}
    plane = [(dx, dy) for dx in range(4) for dy in range(2) if (dx, dy) != (0, 0)]

    def at(dx, dy):
        where_to = {}
        if dx:
            where_to["tp"] = lax.rem(t + dx, 4)
        if dy:
            where_to["fsdp"] = fs + 1 - 2 * y
        return where_to

    def remote(src, dst, send, recv, who):
        return pltpu.make_async_remote_copy(
            src_ref=src, dst_ref=dst, send_sem=send, recv_sem=recv, device_id=who, device_id_type=MESH
        )

    def aligned(value, step):
        return pl.multiple_of(value, step)

    loads = [
        pltpu.make_async_copy(grads, gr, ld.at[0]),
        pltpu.make_async_copy(master, m0, ld.at[1]),
        pltpu.make_async_copy(mone, m1, ld.at[2]),
        pltpu.make_async_copy(mtwo, m2, ld.at[3]),
        pltpu.make_async_copy(inputs.at[:, pl.ds(aligned(rep * 1024, 1024), 1024)], xa, ld.at[4]),
    ]
    for load in loads:
        load.start()
    barrier = pltpu.get_barrier_semaphore()
    partners = [sibling, opposite, up, down] + [at(dx, dy) for dx, dy in plane]
    for who in partners:
        pl.semaphore_signal(barrier, inc=1, device_id=who, device_id_type=MESH)
    row_of = lax.broadcasted_iota(jnp.int32, (256, 256), 0)
    col_of = lax.broadcasted_iota(jnp.int32, (256, 256), 1)
    ones[...] = jnp.where(lax.div(row_of, block_width) == lax.div(col_of, block_width), 1.0, 0.0).astype(BF16)
    for q in range(4):
        target = lax.div(row_of, 8) * 32 + t * 8 + lax.rem(row_of, 8)
        sel[:, q * 256:(q + 1) * 256] = jnp.where(target == col_of + q * 256, 1.0, 0.0).astype(BF16)
    acc[...] = jnp.zeros_like(acc)
    loads[0].wait()
    pl.semaphore_wait(barrier, len(partners))

    def copy_a(u):
        return remote(sa.at[u], ra.at[u], sa_s.at[u], sa_r.at[u], sibling)

    def two_groups(hi, cols):
        pair = gr[pl.ds(aligned(hi * 16, 16), 16), cols].astype(F32)
        return pair[0:8], pair[8:16]

    def stage_a(u, carry):
        for h in range(2):
            cols = pl.ds(aligned(h * half + u * UNIT, UNIT), UNIT)
            a0, a1 = two_groups(yh, cols)
            b0, b1 = two_groups(1 - yh, cols)
            kept = jnp.where(first_core, a1, a0)
            sent = jnp.where(first_core, b1, b0)
            sa[u, :, h * UNIT:(h + 1) * UNIT] = jnp.concatenate([kept, sent], axis=0).astype(BF16)
        copy_a(u).start()
        return carry

    lax.fori_loop(0, nu, stage_a, 0)

    loads[4].wait()
    mine = lax.dot_general(xa[...], sel[...], (((1,), (1,)), ((), ())), preferred_element_type=F32).astype(BF16)
    my_rows = pl.ds(aligned(y * 32, 32), 32)
    xs[my_rows, :] = mine
    copy_x = remote(xs.at[my_rows, :], xs.at[my_rows, :], xs_s, xs_r, mate)
    copy_x.start()
    for load in loads[1:4]:
        load.wait()

    def copy_b(u):
        return remote(sb.at[u], rb.at[u], sb_s.at[u], sb_r.at[u], opposite)

    def stage_b(u):
        copy_a(u).wait_recv()
        sends = []
        for h in range(2):
            cols = pl.ds(aligned(h * half + u * UNIT, UNIT), UNIT)
            a0, a1 = two_groups(yh, cols)
            b0, b1 = two_groups(1 - yh, cols)
            got = ra[u, :, h * UNIT:(h + 1) * UNIT].astype(F32)
            keep[u, :, h * UNIT:(h + 1) * UNIT] = jnp.where(first_core, a0, a1) + got[0:8]
            sends.append(jnp.where(first_core, b0, b1) + got[8:16])
        sb[u] = jnp.concatenate(sends, axis=0).astype(BF16)
        copy_b(u).start()

    def copy_y(u):
        return remote(ys.at[u], yr.at[u], ys_s.at[u], ys_r.at[u], mate)

    def copy_p(u, dx, dy):
        mine = t * 2 + y
        choice = y if dy == 0 else 1 - y
        return remote(ps.at[u, choice], pr.at[u, mine], ps_s.at[u, dx * 2 + dy], ps_r.at[u, mine], at(dx, dy))

    def wait_p(u, dx, dy):
        slot = lax.rem(t + dx, 4) * 2 + (y if dy == 0 else 1 - y)
        remote(ps.at[u, 0], pr.at[u, slot], ps_s.at[u, dx * 2 + dy], ps_r.at[u, slot], at(dx, dy)).wait_recv()

    fix_one = 1.0 - beta_one**10
    fix_two = 1.0 - beta_two**10
    sub = lax.broadcasted_iota(jnp.int32, (8, 128), 0)

    def stage_c(u):
        copy_b(u).wait_recv()
        got = rb[u].astype(F32)
        for h in range(2):
            cols = pl.ds(aligned(h * half + u * UNIT, UNIT), UNIT)
            grad = (keep[u, :, h * UNIT:(h + 1) * UNIT] + got[h * 8:(h + 1) * 8]) * 0.25
            new_one = beta_one * m1[:, cols] + (1.0 - beta_one) * grad
            new_two = beta_two * m2[:, cols] + (1.0 - beta_two) * grad * grad
            step_dir = new_one / fix_one / (jnp.sqrt(new_two / fix_two) + 1e-08)
            old = m0[:, cols]
            new = old - learn_rate * (step_dir + decay_rate * old)
            m0[:, cols] = new
            m1[:, cols] = new_one
            m2[:, cols] = new_two
            total = jnp.sum(jnp.abs(new), axis=0, keepdims=True)
            packed = jnp.zeros((8, 128), F32)
            for r in range(8):
                packed = jnp.where(sub == r, total[:, r * 128:(r + 1) * 128], packed)
            ps[u, h] = packed
        pr[u, t * 2 + y] = ps[u, y]
        for dx, dy in plane:
            copy_p(u, dx, dy).start()
        other = m0[:, pl.ds(aligned((1 - y) * half + u * UNIT, UNIT), UNIT)]
        ys[u] = jnp.concatenate([other[:, :UNIT // 2], other[:, UNIT // 2:]], axis=0).astype(BF16)
        copy_y(u).start()

    def stage_d(u):
        for dx, dy in plane:
            wait_p(u, dx, dy)
        levels = []
        for e in range(2):
            total = pr[u, e] + pr[u, 2 + e] + pr[u, 4 + e] + pr[u, 6 + e]
            levels.append(total * (2.5 / 32.0))
        g[z, :, pl.ds(aligned(u * MSG + UNIT, 128), 128)] = jnp.concatenate(levels, axis=0).astype(BF16)
        copy_y(u).wait_recv()
        got = yr[u].astype(F32)
        theirs = jnp.concatenate([got[0:8], got[8:16]], axis=1)
        own = m0[:, pl.ds(aligned(y * half + u * UNIT, UNIT), UNIT)]
        even = jnp.where(first_y, own, theirs)
        odd = jnp.where(first_y, theirs, own)
        g[z, :, pl.ds(aligned(u * MSG, 128), UNIT)] = jnp.concatenate([even, odd], axis=0).astype(BF16)

    def place(c, src):
        return g.at[src, :, pl.ds(aligned(c * MSG, 128), MSG)]

    def ring(c, s, src, way, who):
        return remote(place(c, src), place(c, src), ring_s.at[way, c, s], ring_r.at[c, src], who)

    def arrived(c, src):
        ring(c, 0, src, 0, up).wait_recv()

    def ring_step(c, s):
        below = lax.rem(z + nz - s, nz)
        above = lax.rem(z + s, nz)
        last = nz // 2 - 1
        if s > 0:
            arrived(c, below)
            if s < last:
                ring(c, s, below, 0, up).start()
            arrived(c, above)
        else:
            ring(c, s, below, 0, up).start()
        if s < last:
            ring(c, s, above, 1, down).start()
        else:
            even = lax.rem(c, 2) == 0
            src = jnp.where(even, below, above)
            to = jnp.where(even, lax.rem(fs + 2, nf), lax.rem(fs + nf - 2, nf))
            ring(c, s, src, 0, {"fsdp": to}).start()

    def og_slot(xsrc, ysrc, core):
        return ogb.at[lax.rem(xsrc, 2), pl.ds(aligned(ysrc * 32 + core * 16, 16), 16), :]

    og_from = ograd.at[pl.ds(aligned(k * 16, 16), 16), :]
    og_row = lax.div(t, 2)
    og_number = lax.rem(t, 2) * 2 + y

    def og_send():
        for dx in range(4):
            to = {"tp": lax.rem(t + dx, 4), "fsdp": fs - y + og_row}
            dst = og_slot(t, y, k)
            if dx == 0:
                @pl.when(og_row == y)
                def _():
                    pltpu.make_async_copy(og_from, dst, og_r.at[og_number]).start()

                @pl.when(og_row != y)
                def _():
                    remote(og_from, dst, og_s.at[dx], og_r.at[og_number], to).start()
            else:
                remote(og_from, dst, og_s.at[dx], og_r.at[og_number], to).start()

    def og_share(i):
        slot = og_slot(2 * y + i // 2, i % 2, k)
        return remote(slot, slot, sh_s.at[i], sh_r.at[i], sibling)

    def og_pass():
        for i in range(4):
            slot = og_slot(2 * y + i // 2, i % 2, k)
            local = jnp.logical_and(t == 2 * y + i // 2, y == i % 2)

            @pl.when(local)
            def _():
                pltpu.make_async_copy(og_from, slot, og_r.at[i]).wait()

            @pl.when(jnp.logical_not(local))
            def _():
                remote(og_from, slot, og_s.at[0], og_r.at[i], mate).wait_recv()

            og_share(i).start()

    def og_finish():
        for i in range(4):
            slot = og_slot(2 * y + i // 2, i % 2, 1 - k)
            remote(slot, slot, sh_s.at[i], sh_r.at[i], sibling).wait_recv()
        other_rows = pl.ds(aligned((1 - y) * 32, 32), 32)
        remote(xs.at[other_rows, :], xs.at[other_rows, :], xs_s, xs_r, mate).wait_recv()

    def fo_cols(u, side):
        return pl.ds(aligned(side * half + u * UNIT, UNIT), UNIT)

    def fo_local(u):
        return pltpu.make_async_copy(fo.at[u, my_rows, :], o_fwd.at[:, fo_cols(u, y)], fo_l.at[u])

    def fo_remote(u, side):
        rows = pl.ds(aligned((1 - y) * 32, 32), 32)
        return remote(fo.at[u, rows, :], o_fwd.at[:, fo_cols(u, side)], fo_s.at[u], fo_r.at[u], mate)

    def products(u, low, high):
        levels = g[:, :, pl.ds(aligned(u * MSG + UNIT, 128), 128)].astype(F32).reshape(2 * nz, 8, 128)
        for i in range(low, high):
            b = 4 * u + i
            whole = g[:, :, pl.ds(aligned(u * MSG + i * 256, 128), 256)].reshape(16 * nz, 256)
            wide = whole.astype(F32)
            spread = [
                jnp.broadcast_to(levels[:, r:r + 1, :], (2 * nz, 8, 128)).reshape(16 * nz, 128)
                for r in (2 * i, 2 * i + 1)
            ]
            level = jnp.concatenate(spread, axis=1)
            band = jnp.maximum(jnp.minimum(wide, level), -level).astype(BF16)
            fwd = jnp.dot(xs[...], band, preferred_element_type=F32)
            fo[u, :, i * 256:(i + 1) * 256] = fwd.astype(BF16)
            sums = jnp.dot(jnp.abs(whole), ones[...], preferred_element_type=F32)
            level = sums * (2.5 / 32.0)
            unit = jnp.maximum(jnp.minimum(wide, level), -level).astype(BF16)
            hg = lax.div(b, 2 * nu)
            og = ogb[hg, :, pl.ds(aligned((b - hg * 2 * nu) * 256, 256), 256)]
            acc[hg] += lax.dot_general(og, unit, (((1,), (1,)), ((), ())), preferred_element_type=F32)

    def results(u):
        fo_local(u).start()
        fo_remote(u, y).start()

    outs = [
        pltpu.make_async_copy(m0, o_master, out_s.at[0]),
        pltpu.make_async_copy(m1, o_one, out_s.at[1]),
        pltpu.make_async_copy(m2, o_two, out_s.at[2]),
    ]
    steps = nz // 2
    rounds = (steps + LEAD - 1) // LEAD

    ahead = 3

    def one_round(q, carry):
        def guarded(back, body):
            @pl.when(jnp.logical_and(q >= ahead + back, q < ahead + back + nu))
            def _():
                body(lax.rem(q + 4 * nu - ahead - back, nu))

        def once(number, body):
            pl.when(q == ahead + number)(body)

        def first_products(c):
            arrived(c, lax.rem(z + nz // 2, nz))
            products(c, 0, 2)

        def last_products(c):
            products(c, 2, 4)
            results(c)

        def write_out():
            for out in outs:
                out.start()

        for j in range(LEAD):
            if j == 0:
                guarded(0, stage_d)
            for i in reversed(range(rounds)):
                s = i * LEAD + j
                if s < steps:
                    guarded(i, functools.partial(ring_step, s=s))
            if j == LEAD - 1:
                once(0, og_send)
                once(1, og_pass)
                once(2, og_finish)
                guarded(rounds - 1, first_products)
            if j == 0:
                guarded(rounds, last_products)
            if j == 1:
                guarded(-3, stage_b)
            if j == 2:
                guarded(-2, stage_c)
                once(nu - 3, write_out)
        return carry

    lax.fori_loop(0, ahead + nu + rounds - 1, one_round, 0)
    products(nu - 1, 2, 4)
    results(nu - 1)

    for hg in range(2):
        rows = acc[hg].astype(BF16)
        bs[hg] = jnp.dot(rows, sel[...], preferred_element_type=F32).astype(BF16)

    def bw_send(hg, yy):
        return remote(
            bs.at[hg, pl.ds(yy * 32, 32), :], br.at[t], bw_s.at[hg * 2 + yy], bw_r.at[t],
            {"tp": 2 * y + hg, "fsdp": fs - y + yy},
        )

    def is_self(hg, yy):
        return jnp.logical_and(t == 2 * y + hg, y == yy)

    for hg in range(2):
        for yy in range(2):
            @pl.when(is_self(hg, yy))
            def _():
                br[t] = bs[hg, yy * 32:(yy + 1) * 32, :]

            @pl.when(jnp.logical_not(is_self(hg, yy)))
            def _():
                bw_send(hg, yy).start()

    at_home = lax.div(t, 2) == y
    for x in range(4):
        @pl.when(jnp.logical_not(jnp.logical_and(at_home, t == x)))
        def _():
            remote(
                bs.at[0, pl.ds(0, 32), :], br.at[x], bw_s.at[0], bw_r.at[x], mate
            ).wait_recv()
    total = br[0].astype(F32) + br[1].astype(F32) + br[2].astype(F32) + br[3].astype(F32)
    bo[...] = total.astype(BF16)
    out_b = pltpu.make_async_copy(bo, o_bwd, out_s.at[3])
    out_b.start()

    for hg in range(2):
        for yy in range(2):
            @pl.when(jnp.logical_not(is_self(hg, yy)))
            def _():
                bw_send(hg, yy).wait_send()
    for dx in range(4):
        def og_done():
            remote(og_from, og_slot(t, y, k), og_s.at[dx], og_r.at[og_number], mate).wait_send()
        if dx == 0:
            pl.when(og_row != y)(og_done)
        else:
            og_done()
    for i in range(4):
        og_share(i).wait_send()
    copy_x.wait_send()

    def finish(u, carry):
        copy_a(u).wait_send()
        copy_b(u).wait_send()
        copy_y(u).wait_send()
        for dx, dy in plane:
            copy_p(u, dx, dy).wait_send()
        for s in range(steps):
            ring(u, s, z, 0, up).wait_send()
            if s < steps - 1:
                ring(u, s, z, 1, down).wait_send()
        fo_local(u).wait()
        fo_remote(u, y).wait_send()
        fo_remote(u, 1 - y).wait_recv()
        return carry

    lax.fori_loop(0, nu, finish, 0)
    for out in outs:
        out.wait()
    out_b.wait()


def local(master, moment_one, moment_two, grads, inputs, out_grad):
    nz = lax.axis_size("fsdp") // 2
    rows, hidden = master.shape[1:]
    tokens = inputs.shape[0]
    nu = hidden // 2 // UNIT
    steps = nz // 2
    any_spec = pl.BlockSpec(memory_space=pl.ANY)
    vm = pltpu.VMEM
    dma = pltpu.SemaphoreType.DMA
    new_master, new_one, new_two, fwd, bwd = pl.pallas_call(
        functools.partial(kernel, nz, nu),
        out_shape=(
            jax.ShapeDtypeStruct((rows, hidden), F32),
            jax.ShapeDtypeStruct((rows, hidden), F32),
            jax.ShapeDtypeStruct((rows, hidden), F32),
            jax.ShapeDtypeStruct((tokens, hidden), BF16),
            jax.ShapeDtypeStruct((tokens, 64 * nz), BF16),
        ),
        in_specs=[any_spec] * 6,
        out_specs=[any_spec] * 5,
        scratch_shapes=[
            vm((rows, hidden), F32),
            vm((rows, hidden), F32),
            vm((rows, hidden), F32),
            vm((32, hidden), BF16),
            vm((tokens, 64 * nz), BF16),
            vm((2 * tokens, 16 * nz), BF16),
            vm((2, 2 * tokens, hidden // 4), BF16),
            vm((16 * nz, 64 * nz), BF16),
            vm((256, 256), BF16),
            vm((nu, 16, 2 * UNIT), BF16),
            vm((nu, 16, 2 * UNIT), BF16),
            vm((nu, 8, 2 * UNIT), F32),
            vm((nu, 16, UNIT), BF16),
            vm((nu, 16, UNIT), BF16),
            vm((nu, 16, UNIT // 2), BF16),
            vm((nu, 16, UNIT // 2), BF16),
            vm((nu, 2, 8, 128), F32),
            vm((nu, 8, 8, 128), F32),
            vm((nz, 16, nu * MSG), BF16),
            vm((nu, 2 * tokens, UNIT), BF16),
            vm((2, 2 * tokens, 16 * nz), F32),
            vm((2, 2 * tokens, 64 * nz), BF16),
            vm((4, tokens, 64 * nz), BF16),
            vm((tokens, 64 * nz), BF16),
            dma((5,)),
            dma((nu,)), dma((nu,)), dma((nu,)), dma((nu,)), dma((nu,)), dma((nu,)),
            dma((nu, 8)), dma((nu, 8)),
            dma((2, nu, steps)), dma((nu, nz)),
            dma((4,)), dma((4,)), dma((4,)), dma((4,)),
            dma, dma,
            dma((nu,)), dma((nu,)), dma((nu,)),
            dma((4,)), dma((4,)),
            dma((4,)),
        ],
        compiler_params=pltpu.CompilerParams(
            collective_id=0, has_side_effects=True, vmem_limit_bytes=48 * 1024 * 1024
        ),
    )(
        master.reshape(rows, hidden),
        moment_one.reshape(rows, hidden),
        moment_two.reshape(rows, hidden),
        grads.reshape(32, hidden),
        inputs,
        out_grad,
    )
    return (
        new_master.reshape(master.shape),
        new_one.reshape(master.shape),
        new_two.reshape(master.shape),
        fwd.reshape(1, 1, tokens, hidden),
        bwd.reshape(1, tokens, 64 * nz),
    )


def solution(mesh):
    placed = (
        P(("rep", "fsdp"), "tp", None),
        P(("rep", "fsdp"), "tp", None),
        P(("rep", "fsdp"), "tp", None),
        P("rep", None, "fsdp", "tp", None),
        P("fsdp", None),
        P("fsdp", "tp"),
    )
    return jax.shard_map(
        local,
        mesh=mesh,
        in_specs=placed,
        out_specs=(
            P(("rep", "fsdp"), "tp", None),
            P(("rep", "fsdp"), "tp", None),
            P(("rep", "fsdp"), "tp", None),
            P("rep", "tp", "fsdp", None),
            P("tp", "fsdp", "rep"),
        ),
        check_vma=False,
    )
```

time: 445 us -> 138 us (0.31)
  waiting for transfers between devices: 248 us -> 0 us
  Pallas kernels: 0 us -> 126 us
  other arithmetic: 107 us -> 0 us
  local copies, waits for them, and re-layouts: 39.9 us -> 9.97 us
  blocking collectives: 25 us -> 0 us
  between operations: 13.9 us -> 0.66 us
  matrix products: 11.4 us -> 0 us
    all_gather x2 -> x0, waiting for transfers between devices: 193 us -> none  [the longest x1 171 us: local(): piece = lax.all_gather(unit_copy, 'fsdp', axis=0, tiled=True)]
    pallas_call x0 -> x1, Pallas kernels: none -> 126 us  [local(): pl.pallas_call(functools.partial(kernel, nz, nu), out_shape=(jax.ShapeDty...]
    unnamed x1 -> x0, other arithmetic: 79.7 us -> none
    reduce_scatter x1 -> x0, waiting for transfers between devices: 54.1 us -> none  [local(): lax.psum_scatter(grads.astype(jnp.float32).astype(jnp.bfloat16), 'rep', s...]
    convert_element_type x3 -> x0, local copies, waits for them, and re-layouts: 15.9 us -> none  [the longest x1 11.5 us: local(): new_master.astype(jnp.bfloat16)]
    psum x1 -> x0, blocking collectives: 14.6 us -> none  [local(): lax.psum(partial_sums.astype(jnp.bfloat16), 'tp').astype(jnp.float32)]
    convert_element_type x4 -> x0, other arithmetic: 13.9 us -> none  [the longest x1 9.73 us: local(): tiles = lax.all_to_all(new_master.astype(jnp.bfloat16), 'tp', split_axis=...]
    abs x1 -> x0, other arithmetic: 12.2 us -> none  [unit_clip(): unit_level = 2.5 * jnp.mean(jnp.abs(blocks), axis=3, keepdims=True)]
  transfers between devices with their start and end apart: 3 -> 0, of which waited for: 3 -> 0; matrix products, arithmetic and copies ran while one was open for 33% -> 0% of each run, Pallas kernels for 0% -> 0%
where the time goes in v1:
time: 138 us; the launch traced here: 137 us
  Pallas kernels  126 us (91%)
  local copies, waits for them, and re-layouts  9.97 us (7%)
    pallas_call x1, Pallas kernels, local(): pl.pallas_call(functools.partial(kernel, nz, nu), out_shape=(jax.ShapeDty...  126 us
    unnamed x17, local copies, waits for them, and re-layouts  9.97 us

profile of v1, /device:TPU:6, one launch (start us, length us, event | category | flops | bytes accessed | tf_op | source)
XLA Modules:
  0.0 136.8 jit_solution(12445652281161203638)
XLA Ops:
  0.6 0.0 copy-start
  0.6 1.2 copy-done
  1.8 0.0 copy-start.1
  1.8 1.0 copy-done.1
  2.8 0.0 copy-start.2
  2.8 1.0 copy-done.2
  3.9 0.0 copy-start.3
  3.9 1.0 copy-done.3
  4.9 0.0 copy-start.4
  4.9 0.9 copy-done.4
  5.8 0.0 copy-start.5
  5.8 0.9 copy-done.5
  6.8 126.1 %shard_map.101 = (f32[8,14336]{1,0:T(8,128)S(1)}, f32[8,14336]{1,0:T(8,128)S(1)}, f32[8,14336]{1,0:T(8,128)S(1)}, bf16[32,14336]{1,0:T(8,128)(2,1)S(1)}, bf16[32,1024]{1,0:T(8,128)(2,1)S(1)}) custom-call(f32[8,14336]{1,0:T(8,128)S(1)} %bitcast.14, f32[8,14336]{1,0:T(8,128)S(1)} %bitcast.15, f32[8,14336]{1,0:T(8,128)S(1)} %bitcast.16, ...), custom_call_target="tpu_custom_call" | custom-call | tf_op jit(solution)/shard_map/pallas_call | solution.py:443
  132.9 0.8 copy.16
  133.7 0.8 copy.17
  134.5 0.8 copy.18
  135.2 0.9 copy.19
  136.1 0.6 copy.20
Async XLA Ops:
  0.6 1.2 copy-start
  1.8 1.0 copy-start.1
  2.8 1.0 copy-start.2
  3.9 1.0 copy-start.3
  4.9 0.9 copy-start.4
  5.8 0.9 copy-start.5

commit v2 on v1

v2 whole, which is shorter than its diff:
```python
import functools

import jax
import jax.numpy as jnp
from jax import lax
from jax.experimental import pallas as pl
from jax.experimental.pallas import tpu as pltpu
from jax.sharding import PartitionSpec as P

beta_one = 0.9
beta_two = 0.95
learn_rate = 0.003
decay_rate = 0.1
block_width = 32

MESH = pl.DeviceIdType.MESH
F32 = jnp.float32
BF16 = jnp.bfloat16

VMEM_BYTES = 63 * 1024 * 1024
UNIT = 1792
BLOCKS = UNIT // 256
MSG = UNIT + 256


def kernel(
    nz, nu,
    master, mone, mtwo, grads, inputs, ograd,
    o_master, o_one, o_two, o_fwd, o_bwd,
    m0, m1, m2, gr, xa, xs, xk, ogb, sel, ones,
    sa, ra, keep, sb, rb, ys, yr, ps, pr, g, facc, fo, acc, bs, br, bo,
    ld, sa_s, sa_r, sb_s, sb_r, ys_s, ys_r, ps_s, ps_r, ring_s, ring_r,
    og_s, og_r, sh_s, sh_r, xs_s, xs_r, fo_s, fo_r, fo_l, bw_s, bw_r, out_s,
):
    half = nu * UNIT
    rep = lax.axis_index("rep")
    fs = lax.axis_index("fsdp")
    t = lax.axis_index("tp")
    nf = 2 * nz
    yh = lax.div(rep, 2)
    k = lax.rem(rep, 2)
    z = lax.div(fs, 2)
    y = lax.rem(fs, 2)
    first_core = k == 0
    first_y = y == 0

    sibling = {"rep": rep + 1 - 2 * k}
    opposite = {"rep": lax.rem(rep + 2, 4)}
    up = {"fsdp": lax.rem(fs + 2, nf)}
    down = {"fsdp": lax.rem(fs + nf - 2, nf)}
    mate = {"fsdp": fs + 1 - 2 * y}
    plane = [(dx, dy) for dx in range(4) for dy in range(2) if (dx, dy) != (0, 0)]

    def at(dx, dy):
        where_to = {}
        if dx:
            where_to["tp"] = lax.rem(t + dx, 4)
        if dy:
            where_to["fsdp"] = fs + 1 - 2 * y
        return where_to

    def remote(src, dst, send, recv, who):
        return pltpu.make_async_remote_copy(
            src_ref=src, dst_ref=dst, send_sem=send, recv_sem=recv, device_id=who, device_id_type=MESH
        )

    def aligned(value, step):
        return pl.multiple_of(value, step)

    loads = [
        pltpu.make_async_copy(grads, gr, ld.at[0]),
        pltpu.make_async_copy(master, m0, ld.at[1]),
        pltpu.make_async_copy(mone, m1, ld.at[2]),
        pltpu.make_async_copy(mtwo, m2, ld.at[3]),
        pltpu.make_async_copy(inputs.at[:, pl.ds(aligned(rep * 1024, 1024), 1024)], xa, ld.at[4]),
    ]
    barrier = pltpu.get_barrier_semaphore()
    partners = [sibling, opposite, up, down] + [at(dx, dy) for dx, dy in plane]
    for who in partners:
        pl.semaphore_signal(barrier, inc=1, device_id=who, device_id_type=MESH)
    for load in loads:
        load.start()
    loads[0].wait()
    pl.semaphore_wait(barrier, len(partners))

    def copy_a(u):
        return remote(sa.at[u], ra.at[u], sa_s.at[u], sa_r.at[u], sibling)

    def two_groups(hi, cols):
        pair = gr[pl.ds(aligned(hi * 16, 16), 16), cols].astype(F32)
        return pair[0:8], pair[8:16]

    def stage_a(u, carry):
        for h in range(2):
            cols = pl.ds(aligned(h * half + u * UNIT, 256), UNIT)
            a0, a1 = two_groups(yh, cols)
            b0, b1 = two_groups(1 - yh, cols)
            kept = jnp.where(first_core, a1, a0)
            sent = jnp.where(first_core, b1, b0)
            sa[u, :, h * UNIT:(h + 1) * UNIT] = jnp.concatenate([kept, sent], axis=0).astype(BF16)
        copy_a(u).start()
        return carry

    lax.fori_loop(0, nu, stage_a, 0)

    my_rows = pl.ds(aligned(y * 32, 32), 32)
    copy_x = remote(xs.at[my_rows, :], xs.at[my_rows, :], xs_s, xs_r, mate)

    def choose():
        row_of = lax.broadcasted_iota(jnp.int32, (256, 256), 0)
        col_of = lax.broadcasted_iota(jnp.int32, (256, 256), 1)
        ones[...] = jnp.where((row_of >> 5) == (col_of >> 5), 1.0, 0.0).astype(BF16)
        slot = row_of >> 4
        away = (slot + 1) >> 1
        band = 2 * (jnp.where((slot & 1) == 1, z + nz - away, z + away) & (nz - 1)) + ((row_of >> 3) & 1)
        target = band * 32 + t * 8 + (row_of & 7)
        for q in range(4):
            sel[:, q * 256:(q + 1) * 256] = jnp.where(target == col_of + q * 256, 1.0, 0.0).astype(BF16)
        acc[...] = jnp.zeros_like(acc)
        loads[4].wait()
        mine = lax.dot_general(xa[...], sel[...], (((1,), (1,)), ((), ())), preferred_element_type=F32)
        xs[my_rows, :] = mine.astype(BF16)
        copy_x.start()

    def copy_b(u):
        return remote(sb.at[u], rb.at[u], sb_s.at[u], sb_r.at[u], opposite)

    def stage_b(u):
        copy_a(u).wait_recv()
        sends = []
        for h in range(2):
            cols = pl.ds(aligned(h * half + u * UNIT, 256), UNIT)
            a0, a1 = two_groups(yh, cols)
            b0, b1 = two_groups(1 - yh, cols)
            got = ra[u, :, h * UNIT:(h + 1) * UNIT].astype(F32)
            keep[u, :, h * UNIT:(h + 1) * UNIT] = jnp.where(first_core, a0, a1) + got[0:8]
            sends.append(jnp.where(first_core, b0, b1) + got[8:16])
        sb[u] = jnp.concatenate(sends, axis=0).astype(BF16)
        copy_b(u).start()

    def copy_y(u):
        return remote(ys.at[u], yr.at[u], ys_s.at[u], ys_r.at[u], mate)

    def copy_p(u, dx, dy):
        mine = t * 2 + y
        choice = y if dy == 0 else 1 - y
        return remote(ps.at[u, choice], pr.at[u, mine], ps_s.at[u, dx * 2 + dy], ps_r.at[u, mine], at(dx, dy))

    def wait_p(u, dx, dy):
        slot = lax.rem(t + dx, 4) * 2 + (y if dy == 0 else 1 - y)
        remote(ps.at[u, 0], pr.at[u, slot], ps_s.at[u, dx * 2 + dy], ps_r.at[u, slot], at(dx, dy)).wait_recv()

    scale_one = 1.0 / (1.0 - beta_one**10)
    scale_two = 1.0 / (1.0 - beta_two**10)
    sub = lax.broadcasted_iota(jnp.int32, (8, 256), 0)

    def stage_c(u):
        copy_b(u).wait_recv()
        got = rb[u].astype(F32)
        for h in range(2):
            cols = pl.ds(aligned(h * half + u * UNIT, 256), UNIT)
            grad = (keep[u, :, h * UNIT:(h + 1) * UNIT] + got[h * 8:(h + 1) * 8]) * 0.25
            new_one = beta_one * m1[:, cols] + (1.0 - beta_one) * grad
            new_two = beta_two * m2[:, cols] + (1.0 - beta_two) * grad * grad
            step_dir = new_one * scale_one / (jnp.sqrt(new_two * scale_two) + 1e-08)
            old = m0[:, cols]
            new = old - learn_rate * (step_dir + decay_rate * old)
            m0[:, cols] = new
            m1[:, cols] = new_one
            m2[:, cols] = new_two
            total = jnp.sum(jnp.abs(new), axis=0, keepdims=True)
            packed = jnp.zeros((8, 256), F32)
            for r in range(BLOCKS):
                packed = jnp.where(sub == r, total[:, r * 256:(r + 1) * 256], packed)
            ps[u, h] = packed
        pr[u, t * 2 + y] = ps[u, y]
        for dx, dy in plane:
            copy_p(u, dx, dy).start()
        other = m0[:, pl.ds(aligned((1 - y) * half + u * UNIT, 256), UNIT)]
        ys[u] = jnp.concatenate([other[:, :UNIT // 2], other[:, UNIT // 2:]], axis=0).astype(BF16)
        copy_y(u).start()

    def stage_d(u):
        for dx, dy in plane:
            wait_p(u, dx, dy)
        levels = []
        for e in range(2):
            total = pr[u, e] + pr[u, 2 + e] + pr[u, 4 + e] + pr[u, 6 + e]
            levels.append(total * (2.5 / 32.0))
        g[0, :, pl.ds(aligned(u * MSG + UNIT, 256), 256)] = jnp.concatenate(levels, axis=0).astype(BF16)
        copy_y(u).wait_recv()
        got = yr[u].astype(F32)
        theirs = jnp.concatenate([got[0:8], got[8:16]], axis=1)
        own = m0[:, pl.ds(aligned(y * half + u * UNIT, 256), UNIT)]
        even = jnp.where(first_y, own, theirs)
        odd = jnp.where(first_y, theirs, own)
        g[0, :, pl.ds(aligned(u * MSG, 128), UNIT)] = jnp.concatenate([even, odd], axis=0).astype(BF16)

    def place(c, slot):
        return g.at[slot, :, pl.ds(aligned(c * MSG, 128), MSG)]

    def ring(c, s, way, who):
        src = max(2 * s - 1, 0) if way == 0 else 2 * s
        dst = min(2 * s + 1 + way, nz - 1)
        return remote(place(c, src), place(c, dst), ring_s.at[way, c, s], ring_r.at[c, dst], who)

    def arrived(c, slot):
        remote(place(c, slot), place(c, slot), ring_s.at[0, c, 0], ring_r.at[c, slot], up).wait_recv()

    def ring_step(c, s):
        if s > 0:
            arrived(c, 2 * s - 1)
        if s < steps - 1:
            ring(c, s, 0, up).start()
            if s > 0:
                arrived(c, 2 * s)
            ring(c, s, 1, down).start()
        else:
            arrived(c, 2 * s)

            @pl.when(lax.rem(c, 2) == 0)
            def _():
                ring(c, s, 0, up).start()

            @pl.when(lax.rem(c, 2) == 1)
            def _():
                ring(c, s, 1, down).start()

    def og_slot(xsrc, ysrc, core):
        return ogb.at[lax.rem(xsrc, 2), pl.ds(aligned(ysrc * 32 + core * 16, 16), 16), :]

    og_from = ograd.at[pl.ds(aligned(k * 16, 16), 16), :]
    og_row = lax.div(t, 2)
    og_number = lax.rem(t, 2) * 2 + y

    def og_send():
        for dx in range(4):
            to = {"tp": lax.rem(t + dx, 4), "fsdp": fs - y + og_row}
            dst = og_slot(t, y, k)
            if dx == 0:
                @pl.when(og_row == y)
                def _():
                    pltpu.make_async_copy(og_from, dst, og_r.at[og_number]).start()

                @pl.when(og_row != y)
                def _():
                    remote(og_from, dst, og_s.at[dx], og_r.at[og_number], to).start()
            else:
                remote(og_from, dst, og_s.at[dx], og_r.at[og_number], to).start()

    def og_share(i):
        slot = og_slot(2 * y + i // 2, i % 2, k)
        return remote(slot, slot, sh_s.at[i], sh_r.at[i], sibling)

    def og_pass():
        for i in range(4):
            slot = og_slot(2 * y + i // 2, i % 2, k)
            local = jnp.logical_and(t == 2 * y + i // 2, y == i % 2)

            @pl.when(local)
            def _():
                pltpu.make_async_copy(og_from, slot, og_r.at[i]).wait()

            @pl.when(jnp.logical_not(local))
            def _():
                remote(og_from, slot, og_s.at[0], og_r.at[i], mate).wait_recv()

            og_share(i).start()

    def og_finish():
        for i in range(4):
            slot = og_slot(2 * y + i // 2, i % 2, 1 - k)
            remote(slot, slot, sh_s.at[i], sh_r.at[i], sibling).wait_recv()
        other_rows = pl.ds(aligned((1 - y) * 32, 32), 32)
        remote(xs.at[other_rows, :], xs.at[other_rows, :], xs_s, xs_r, mate).wait_recv()
        for kk in range(4):
            xk[kk] = xs[:, kk * 64:(kk + 1) * 64]

    def fo_cols(u, side):
        return pl.ds(aligned(side * half + u * UNIT, 256), UNIT)

    def fo_local(u):
        return pltpu.make_async_copy(fo.at[u, my_rows, :], o_fwd.at[:, fo_cols(u, y)], fo_l.at[u])

    def fo_remote(u, side):
        rows = pl.ds(aligned((1 - y) * 32, 32), 32)
        return remote(fo.at[u, rows, :], o_fwd.at[:, fo_cols(u, side)], fo_s.at[u], fo_r.at[u], mate)

    def products(u, kk):
        slots = slice(4 * kk, 4 * kk + 4)
        levels = g[slots, :, pl.ds(aligned(u * MSG + UNIT, 256), 256)].astype(F32).reshape(8, 8, 256)
        wholes = [g[slots, :, pl.ds(aligned(u * MSG + i * 256, 256), 256)].reshape(64, 256) for i in range(BLOCKS)]
        sums = jnp.dot(jnp.abs(jnp.concatenate(wholes, axis=0)), ones[...], preferred_element_type=F32)
        hg = lax.div(u, 2)
        for i in range(BLOCKS):
            wide = wholes[i].astype(F32)
            level = jnp.broadcast_to(levels[:, i:i + 1, :], (8, 8, 256)).reshape(64, 256)
            band = jnp.maximum(jnp.minimum(wide, level), -level).astype(BF16)
            fwd = jnp.dot(xk[kk], band, preferred_element_type=F32)
            cols = slice(i * 256, (i + 1) * 256)
            if kk == 0:
                facc[u, :, cols] = fwd
            elif kk < 3:
                facc[u, :, cols] += fwd
            else:
                fo[u, :, cols] = (facc[u, :, cols] + fwd).astype(BF16)
            level = sums[i * 64:(i + 1) * 64] * (2.5 / 32.0)
            unit = jnp.maximum(jnp.minimum(wide, level), -level).astype(BF16)
            og = ogb[hg, :, pl.ds(aligned(lax.rem(u, 2) * UNIT + i * 256, 256), 256)]
            acc[hg, kk * 64:(kk + 1) * 64, :] += lax.dot_general(
                unit, og, (((1,), (1,)), ((), ())), preferred_element_type=F32
            )

    def results(u):
        fo_local(u).start()
        fo_remote(u, y).start()

    outs = [
        pltpu.make_async_copy(m0, o_master, out_s.at[0]),
        pltpu.make_async_copy(m1, o_one, out_s.at[1]),
        pltpu.make_async_copy(m2, o_two, out_s.at[2]),
    ]
    steps = nz // 2

    def bw_send(hg, yy):
        return remote(
            bs.at[hg, pl.ds(yy * 32, 32), :], br.at[t], bw_s.at[hg * 2 + yy], bw_r.at[t],
            {"tp": 2 * y + hg, "fsdp": fs - y + yy},
        )

    def is_self(hg, yy):
        return jnp.logical_and(t == 2 * y + hg, y == yy)

    def backward(hg):
        bs[hg] = lax.dot_general(
            acc[hg].astype(BF16), sel[...], (((0,), (0,)), ((), ())), preferred_element_type=F32
        ).astype(BF16)
        for yy in range(2):
            @pl.when(is_self(hg, yy))
            def _():
                br[t] = bs[hg, yy * 32:(yy + 1) * 32, :]

            @pl.when(jnp.logical_not(is_self(hg, yy)))
            def _():
                bw_send(hg, yy).start()

    def finish_early(u, carry):
        copy_a(u).wait_send()
        copy_b(u).wait_send()
        copy_y(u).wait_send()
        for dx, dy in plane:
            copy_p(u, dx, dy).wait_send()
        return carry

    def finish_ring(u, carry):
        for s in range(steps - 1):
            ring(u, s, 0, up).wait_send()
            ring(u, s, 1, down).wait_send()
        pl.when(lax.rem(u, 2) == 0)(lambda: ring(u, steps - 1, 0, up).wait_send())
        pl.when(lax.rem(u, 2) == 1)(lambda: ring(u, steps - 1, 1, down).wait_send())
        return carry

    def finish_late(u, carry):
        fo_local(u).wait()
        fo_remote(u, y).wait_send()
        fo_remote(u, 1 - y).wait_recv()
        return carry

    def each(low, high, body):
        def step(c, carry):
            body(c)
            return carry

        lax.fori_loop(low, high, step, 0)

    def start_piece(c):
        stage_d(c)
        ring_step(c, 0)

        @pl.when(c + 2 < nu)
        def _():
            stage_c(lax.rem(c + 2, nu))

    def finish_piece(c):
        arrived(c, nz - 1)
        products(c, 3)
        results(c)

    def last_steps(q, carry):
        def guarded(back, body):
            @pl.when(jnp.logical_and(q >= back, q < back + nu))
            def _():
                body(lax.rem(q + 2 * nu - back, nu))

        guarded(0, functools.partial(ring_step, s=steps - 2))
        guarded(1, functools.partial(ring_step, s=steps - 1))
        guarded(1, functools.partial(products, kk=2))
        guarded(2, finish_piece)
        pl.when(q == nu // 2 + 1)(functools.partial(backward, 0))
        return carry

    each(0, 2, stage_b)
    choose()
    each(2, nu, stage_b)
    for load in loads[1:4]:
        load.wait()
    stage_c(0)
    stage_c(1)
    each(0, nu, start_piece)
    for out in outs:
        out.start()
    og_send()
    for s in range(1, steps - 2):
        each(0, nu, functools.partial(ring_step, s=s))
        if s == 1:
            lax.fori_loop(0, nu, finish_early, 0)
            copy_x.wait_send()
        if s == 3:
            og_pass()
        if s == 4:
            og_finish()
            each(0, nu, functools.partial(products, kk=0))
        if s == 5:
            each(0, nu, functools.partial(products, kk=1))
    lax.fori_loop(0, nu + 2, last_steps, 0)
    backward(1)
    lax.fori_loop(0, nu, finish_ring, 0)
    for out in outs:
        out.wait()

    at_home = lax.div(t, 2) == y
    for x in range(4):
        @pl.when(jnp.logical_not(jnp.logical_and(at_home, t == x)))
        def _():
            remote(
                bs.at[0, pl.ds(0, 32), :], br.at[x], bw_s.at[0], bw_r.at[x], mate
            ).wait_recv()
    total = br[0].astype(F32) + br[1].astype(F32) + br[2].astype(F32) + br[3].astype(F32)
    bo[...] = total.astype(BF16)
    out_b = pltpu.make_async_copy(bo, o_bwd, out_s.at[3])
    out_b.start()

    for hg in range(2):
        for yy in range(2):
            @pl.when(jnp.logical_not(is_self(hg, yy)))
            def _():
                bw_send(hg, yy).wait_send()
    for dx in range(4):
        def og_done():
            remote(og_from, og_slot(t, y, k), og_s.at[dx], og_r.at[og_number], mate).wait_send()
        if dx == 0:
            pl.when(og_row != y)(og_done)
        else:
            og_done()
    for i in range(4):
        og_share(i).wait_send()
    lax.fori_loop(0, nu, finish_late, 0)
    out_b.wait()


def hand_over(*refs):
    ins, outs, held, came, went = refs[:5], refs[5:10], refs[10:15], refs[15], refs[16]
    reads = [pltpu.make_async_copy(ins[i], held[i], came.at[i]) for i in range(5)]
    writes = [pltpu.make_async_copy(held[i], outs[i], went.at[i]) for i in range(5)]
    for copy in reads:
        copy.start()
    for read, write in zip(reads, writes):
        read.wait()
        write.start()
    for copy in writes:
        copy.wait()


def local(master, moment_one, moment_two, grads, inputs, out_grad):
    nz = lax.axis_size("fsdp") // 2
    rows, hidden = master.shape[1:]
    tokens = inputs.shape[0]
    nu = hidden // 2 // UNIT
    steps = nz // 2
    any_spec = pl.BlockSpec(memory_space=pltpu.HBM)
    vm = pltpu.VMEM
    dma = pltpu.SemaphoreType.DMA
    results = (
        jax.ShapeDtypeStruct((rows, hidden), F32),
        jax.ShapeDtypeStruct((rows, hidden), F32),
        jax.ShapeDtypeStruct((rows, hidden), F32),
        jax.ShapeDtypeStruct((tokens, hidden), BF16),
        jax.ShapeDtypeStruct((tokens, 64 * nz), BF16),
    )
    made = pl.pallas_call(
        functools.partial(kernel, nz, nu),
        out_shape=results,
        in_specs=[any_spec] * 6,
        out_specs=[any_spec] * 5,
        scratch_shapes=[
            vm((rows, hidden), F32),
            vm((rows, hidden), F32),
            vm((rows, hidden), F32),
            vm((32, hidden), BF16),
            vm((tokens, 64 * nz), BF16),
            vm((2 * tokens, 16 * nz), BF16),
            vm((4, 2 * tokens, 64), BF16),
            vm((2, 2 * tokens, hidden // 4), BF16),
            vm((16 * nz, 64 * nz), BF16),
            vm((256, 256), BF16),
            vm((nu, 16, 2 * UNIT), BF16),
            vm((nu, 16, 2 * UNIT), BF16),
            vm((nu, 8, 2 * UNIT), F32),
            vm((nu, 16, UNIT), BF16),
            vm((nu, 16, UNIT), BF16),
            vm((nu, 16, UNIT // 2), BF16),
            vm((nu, 16, UNIT // 2), BF16),
            vm((nu, 2, 8, 256), F32),
            vm((nu, 8, 8, 256), F32),
            vm((nz, 16, nu * MSG), BF16),
            vm((nu, 2 * tokens, UNIT), F32),
            vm((nu, 2 * tokens, UNIT), BF16),
            vm((2, 16 * nz, 2 * tokens), F32),
            vm((2, 2 * tokens, 64 * nz), BF16),
            vm((4, tokens, 64 * nz), BF16),
            vm((tokens, 64 * nz), BF16),
            dma((5,)),
            dma((nu,)), dma((nu,)), dma((nu,)), dma((nu,)), dma((nu,)), dma((nu,)),
            dma((nu, 8)), dma((nu, 8)),
            dma((2, nu, steps)), dma((nu, nz)),
            dma((4,)), dma((4,)), dma((4,)), dma((4,)),
            dma, dma,
            dma((nu,)), dma((nu,)), dma((nu,)),
            dma((4,)), dma((4,)),
            dma((4,)),
        ],
        compiler_params=pltpu.CompilerParams(
            collective_id=0, has_side_effects=True, vmem_limit_bytes=VMEM_BYTES
        ),
    )(
        master.reshape(rows, hidden),
        moment_one.reshape(rows, hidden),
        moment_two.reshape(rows, hidden),
        grads.reshape(32, hidden),
        inputs,
        out_grad,
    )
    new_master, new_one, new_two, fwd, bwd = pl.pallas_call(
        hand_over,
        out_shape=results,
        in_specs=[any_spec] * 5,
        out_specs=[any_spec] * 5,
        scratch_shapes=[vm(made[i].shape, made[i].dtype) for i in range(5)] + [dma((5,)), dma((5,))],
        compiler_params=pltpu.CompilerParams(vmem_limit_bytes=VMEM_BYTES),
    )(*made)
    return (
        new_master.reshape(master.shape),
        new_one.reshape(master.shape),
        new_two.reshape(master.shape),
        fwd.reshape(1, 1, tokens, hidden),
        bwd.reshape(1, tokens, 64 * nz),
    )


def solution(mesh):
    placed = (
        P(("rep", "fsdp"), "tp", None),
        P(("rep", "fsdp"), "tp", None),
        P(("rep", "fsdp"), "tp", None),
        P("rep", None, "fsdp", "tp", None),
        P("fsdp", None),
        P("fsdp", "tp"),
    )
    return jax.shard_map(
        local,
        mesh=mesh,
        in_specs=placed,
        out_specs=(
            P(("rep", "fsdp"), "tp", None),
            P(("rep", "fsdp"), "tp", None),
            P(("rep", "fsdp"), "tp", None),
            P("rep", "tp", "fsdp", None),
            P("tp", "fsdp", "rep"),
        ),
        check_vma=False,
    )
```

time: 138 us -> 87.1 us (0.63)
  Pallas kernels: 126 us -> 85.7 us
  local copies, waits for them, and re-layouts: 9.97 us -> 0 us
    pallas_call x1 -> x2, Pallas kernels: 126 us -> 85.7 us  [the longest x1 83.1 us: local(): pl.pallas_call(functools.partial(kernel, nz, nu), out_shape=results, in_s...]
    unnamed x17 -> x0, local copies, waits for them, and re-layouts: 9.97 us -> none
where the time goes in v2:
time: 87.1 us; the launch traced here: 86.4 us
  Pallas kernels  85.7 us (98%)
    pallas_call x1, Pallas kernels, local(): pl.pallas_call(functools.partial(kernel, nz, nu), out_shape=results, in_s...  83.1 us
    pallas_call x1, Pallas kernels, local(): pl.pallas_call(hand_over, out_shape=results, in_specs=[any_spec] * 5, out...  2.62 us

profile of v2, /device:TPU:6, one launch (start us, length us, event | category | flops | bytes accessed | tf_op | source)
XLA Modules:
  0.0 86.4 jit_solution(8956582705405444651)
XLA Ops:
  0.6 83.1 %shard_map.101 = (f32[8,14336]{1,0:T(8,128)}, f32[8,14336]{1,0:T(8,128)}, f32[8,14336]{1,0:T(8,128)}, bf16[32,14336]{1,0:T(8,128)(2,1)}, bf16[32,1024]{1,0:T(8,128)(2,1)}) custom-call(f32[8,14336]{1,0:T(8,128)} %bitcast.10, f32[8,14336]{1,0:T(8,128)} %bitcast.11, f32[8,14336]{1,0:T(8,128)} %bitcast.12, bf16[32,14336]{1,0:T(8,128)(2,1)} %bitcast.9, ...), custom_call_target="tpu_custom_call" | custom-call | tf_op jit(solution)/shard_map/pallas_call | solution.py:490
  83.7 2.6 %shard_map.102 = (f32[8,14336]{1,0:T(8,128)}, f32[8,14336]{1,0:T(8,128)}, f32[8,14336]{1,0:T(8,128)}, bf16[32,14336]{1,0:T(8,128)(2,1)}, bf16[32,1024]{1,0:T(8,128)(2,1)}) custom-call(f32[8,14336]{1,0:T(8,128)} %get-tuple-element.15.refs_0_, f32[8,14336]{1,0:T(8,128)} %get-tuple-element.16.refs_1_, f32[8,14336]{1,0:T(8,128)} %get-tuple-element.17.refs_2_, ...), custom_call_target="tpu_custom_call" | custom-call | tf_op jit(solution)/shard_map/pallas_call | solution.py:543

commit v3 on v2

--- a/solution.py
+++ b/solution.py
@@ -20,6 +20,7 @@
 VMEM_BYTES = 63 * 1024 * 1024
 UNIT = 1792
 BLOCKS = UNIT // 256
+PARTS = ((0, 5), (5, 10), (10, 15), (15, 16))
 MSG = UNIT + 256
 
 
@@ -273,8 +274,19 @@
             remote(slot, slot, sh_s.at[i], sh_r.at[i], sibling).wait_recv()
         other_rows = pl.ds(aligned((1 - y) * 32, 32), 32)
         remote(xs.at[other_rows, :], xs.at[other_rows, :], xs_s, xs_r, mate).wait_recv()
-        for kk in range(4):
-            xk[kk] = xs[:, kk * 64:(kk + 1) * 64]
+        for kk, (low, high) in enumerate(PARTS):
+            xk[kk, :, :16 * (high - low)] = xs[:, 16 * low:16 * high]
+
+    def og_sent():
+        for dx in range(4):
+            def og_done():
+                remote(og_from, og_slot(t, y, k), og_s.at[dx], og_r.at[og_number], mate).wait_send()
+            if dx == 0:
+                pl.when(og_row != y)(og_done)
+            else:
+                og_done()
+        for i in range(4):
+            og_share(i).wait_send()
 
     def fo_cols(u, side):
         return pl.ds(aligned(side * half + u * UNIT, 256), UNIT)
@@ -287,27 +299,28 @@
         return remote(fo.at[u, rows, :], o_fwd.at[:, fo_cols(u, side)], fo_s.at[u], fo_r.at[u], mate)
 
     def products(u, kk):
-        slots = slice(4 * kk, 4 * kk + 4)
-        levels = g[slots, :, pl.ds(aligned(u * MSG + UNIT, 256), 256)].astype(F32).reshape(8, 8, 256)
-        wholes = [g[slots, :, pl.ds(aligned(u * MSG + i * 256, 256), 256)].reshape(64, 256) for i in range(BLOCKS)]
+        low, high = PARTS[kk]
+        slots, rows, bands = slice(low, high), 16 * (high - low), 2 * (high - low)
+        levels = g[slots, :, pl.ds(aligned(u * MSG + UNIT, 256), 256)].astype(F32).reshape(bands, 8, 256)
+        wholes = [g[slots, :, pl.ds(aligned(u * MSG + i * 256, 256), 256)].reshape(rows, 256) for i in range(BLOCKS)]
         sums = jnp.dot(jnp.abs(jnp.concatenate(wholes, axis=0)), ones[...], preferred_element_type=F32)
         hg = lax.div(u, 2)
         for i in range(BLOCKS):
             wide = wholes[i].astype(F32)
-            level = jnp.broadcast_to(levels[:, i:i + 1, :], (8, 8, 256)).reshape(64, 256)
+            level = jnp.broadcast_to(levels[:, i:i + 1, :], (bands, 8, 256)).reshape(rows, 256)
             band = jnp.maximum(jnp.minimum(wide, level), -level).astype(BF16)
-            fwd = jnp.dot(xk[kk], band, preferred_element_type=F32)
+            fwd = jnp.dot(xk[kk, :, :rows], band, preferred_element_type=F32)
             cols = slice(i * 256, (i + 1) * 256)
             if kk == 0:
                 facc[u, :, cols] = fwd
-            elif kk < 3:
+            elif kk < len(PARTS) - 1:
                 facc[u, :, cols] += fwd
             else:
                 fo[u, :, cols] = (facc[u, :, cols] + fwd).astype(BF16)
-            level = sums[i * 64:(i + 1) * 64] * (2.5 / 32.0)
+            level = sums[i * rows:(i + 1) * rows] * (2.5 / 32.0)
             unit = jnp.maximum(jnp.minimum(wide, level), -level).astype(BF16)
             og = ogb[hg, :, pl.ds(aligned(lax.rem(u, 2) * UNIT + i * 256, 256), 256)]
-            acc[hg, kk * 64:(kk + 1) * 64, :] += lax.dot_general(
+            acc[hg, 16 * low:16 * high, :] += lax.dot_general(
                 unit, og, (((1,), (1,)), ((), ())), preferred_element_type=F32
             )
 
@@ -352,10 +365,13 @@
             copy_p(u, dx, dy).wait_send()
         return carry
 
-    def finish_ring(u, carry):
-        for s in range(steps - 1):
+    def sent(u, low, high):
+        for s in range(low, high):
             ring(u, s, 0, up).wait_send()
             ring(u, s, 1, down).wait_send()
+
+    def sent_last(u, carry):
+        sent(u, 4, steps - 1)
         pl.when(lax.rem(u, 2) == 0)(lambda: ring(u, steps - 1, 0, up).wait_send())
         pl.when(lax.rem(u, 2) == 1)(lambda: ring(u, steps - 1, 1, down).wait_send())
         return carry
@@ -377,26 +393,42 @@
         stage_d(c)
         ring_step(c, 0)
 
-        @pl.when(c + 2 < nu)
+        @pl.when(c + 3 < nu)
         def _():
-            stage_c(lax.rem(c + 2, nu))
+            stage_c(lax.rem(c + 3, nu))
 
     def finish_piece(c):
         arrived(c, nz - 1)
         products(c, 3)
         results(c)
 
+    def step_and_waits(c, s):
+        ring_step(c, s)
+        if s == 2:
+            finish_early(c, 0)
+        if s == 3:
+            sent(c, 0, 2)
+
+    def early_sent(c, s):
+        ring_step(c, s)
+        products(c, 2)
+        sent(c, 2, 4)
+
+    def step_and_part(c, s, kk):
+        ring_step(c, s)
+        products(c, kk)
+
     def last_steps(q, carry):
         def guarded(back, body):
             @pl.when(jnp.logical_and(q >= back, q < back + nu))
             def _():
                 body(lax.rem(q + 2 * nu - back, nu))
 
-        guarded(0, functools.partial(ring_step, s=steps - 2))
-        guarded(1, functools.partial(ring_step, s=steps - 1))
-        guarded(1, functools.partial(products, kk=2))
-        guarded(2, finish_piece)
-        pl.when(q == nu // 2 + 1)(functools.partial(backward, 0))
+        guarded(0, functools.partial(step_and_part, s=steps - 3, kk=1))
+        guarded(1, functools.partial(ring_step, s=steps - 2))
+        guarded(2, functools.partial(early_sent, s=steps - 1))
+        guarded(3, finish_piece)
+        pl.when(q == nu // 2 + 2)(functools.partial(backward, 0))
         return carry
 
     each(0, 2, stage_b)
@@ -404,27 +436,25 @@
     each(2, nu, stage_b)
     for load in loads[1:4]:
         load.wait()
-    stage_c(0)
-    stage_c(1)
+    each(0, 3, stage_c)
     each(0, nu, start_piece)
     for out in outs:
         out.start()
     og_send()
-    for s in range(1, steps - 2):
-        each(0, nu, functools.partial(ring_step, s=s))
-        if s == 1:
-            lax.fori_loop(0, nu, finish_early, 0)
+    for s in range(1, steps - 3):
+        if s == steps - 4:
+            og_finish()
+            og_sent()
             copy_x.wait_send()
+        if s >= steps - 4:
+            each(0, nu, functools.partial(step_and_part, s=s, kk=s - steps + 4))
+        else:
+            each(0, nu, functools.partial(step_and_waits, s=s))
         if s == 3:
             og_pass()
-        if s == 4:
-            og_finish()
-            each(0, nu, functools.partial(products, kk=0))
-        if s == 5:
-            each(0, nu, functools.partial(products, kk=1))
-    lax.fori_loop(0, nu + 2, last_steps, 0)
+    lax.fori_loop(0, nu + 3, last_steps, 0)
     backward(1)
-    lax.fori_loop(0, nu, finish_ring, 0)
+    lax.fori_loop(0, nu, sent_last, 0)
     for out in outs:
         out.wait()
 
@@ -445,15 +475,6 @@
             @pl.when(jnp.logical_not(is_self(hg, yy)))
             def _():
                 bw_send(hg, yy).wait_send()
-    for dx in range(4):
-        def og_done():
-            remote(og_from, og_slot(t, y, k), og_s.at[dx], og_r.at[og_number], mate).wait_send()
-        if dx == 0:
-            pl.when(og_row != y)(og_done)
-        else:
-            og_done()
-    for i in range(4):
-        og_share(i).wait_send()
     lax.fori_loop(0, nu, finish_late, 0)
     out_b.wait()
 
@@ -499,7 +520,7 @@
             vm((32, hidden), BF16),
             vm((tokens, 64 * nz), BF16),
             vm((2 * tokens, 16 * nz), BF16),
-            vm((4, 2 * tokens, 64), BF16),
+            vm((4, 2 * tokens, 80), BF16),
             vm((2, 2 * tokens, hidden // 4), BF16),
             vm((16 * nz, 64 * nz), BF16),
             vm((256, 256), BF16),

time: 87.1 us -> 86.3 us (level)
  no operation moved by 1% of the time
where the time goes in v3:
time: 86.3 us; the launch traced here: 86.1 us
  Pallas kernels  85.5 us (99%)
    pallas_call x1, Pallas kernels, local(): pl.pallas_call(functools.partial(kernel, nz, nu), out_shape=results, in_s...  82.9 us
    pallas_call x1, Pallas kernels, local(): pl.pallas_call(hand_over, out_shape=results, in_specs=[any_spec] * 5, out...  2.62 us

profile of v3, /device:TPU:6, one launch (start us, length us, event | category | flops | bytes accessed | tf_op | source)
XLA Modules:
  0.0 86.1 jit_solution(6454297328325926690)
XLA Ops:
  0.6 82.9 %shard_map.101 = (f32[8,14336]{1,0:T(8,128)}, f32[8,14336]{1,0:T(8,128)}, f32[8,14336]{1,0:T(8,128)}, bf16[32,14336]{1,0:T(8,128)(2,1)}, bf16[32,1024]{1,0:T(8,128)(2,1)}) custom-call(f32[8,14336]{1,0:T(8,128)} %bitcast.10, f32[8,14336]{1,0:T(8,128)} %bitcast.11, f32[8,14336]{1,0:T(8,128)} %bitcast.12, bf16[32,14336]{1,0:T(8,128)(2,1)} %bitcast.9, ...), custom_call_target="tpu_custom_call" | custom-call | tf_op jit(solution)/shard_map/pallas_call | solution.py:511
  83.5 2.6 %shard_map.102 = (f32[8,14336]{1,0:T(8,128)}, f32[8,14336]{1,0:T(8,128)}, f32[8,14336]{1,0:T(8,128)}, bf16[32,14336]{1,0:T(8,128)(2,1)}, bf16[32,1024]{1,0:T(8,128)(2,1)}) custom-call(f32[8,14336]{1,0:T(8,128)} %get-tuple-element.15.refs_0_, f32[8,14336]{1,0:T(8,128)} %get-tuple-element.16.refs_1_, f32[8,14336]{1,0:T(8,128)} %get-tuple-element.17.refs_2_, ...), custom_call_target="tpu_custom_call" | custom-call | tf_op jit(solution)/shard_map/pallas_call | solution.py:564

commit v4 on v3

--- a/solution.py
+++ b/solution.py
@@ -28,7 +28,7 @@
     nz, nu,
     master, mone, mtwo, grads, inputs, ograd,
     o_master, o_one, o_two, o_fwd, o_bwd,
-    m0, m1, m2, gr, xa, xs, xk, ogb, sel, ones,
+    m0, m1, m2, gr, xa, xs, xk, ogb, sel, spread_to, eye, ones,
     sa, ra, keep, sb, rb, ys, yr, ps, pr, g, facc, fo, acc, bs, br, bo,
     ld, sa_s, sa_r, sb_s, sb_r, ys_s, ys_r, ps_s, ps_r, ring_s, ring_r,
     og_s, og_r, sh_s, sh_r, xs_s, xs_r, fo_s, fo_r, fo_l, bw_s, bw_r, out_s,
@@ -107,16 +107,28 @@
     my_rows = pl.ds(aligned(y * 32, 32), 32)
     copy_x = remote(xs.at[my_rows, :], xs.at[my_rows, :], xs_s, xs_r, mate)
 
+    def place_columns(ref, x):
+        row_of = lax.broadcasted_iota(jnp.int32, (256, 256), 0)
+        col_of = lax.broadcasted_iota(jnp.int32, (256, 256), 1)
+        slot = row_of >> 4
+        away = (slot + 1) >> 1
+        band = 2 * (jnp.where((slot & 1) == 1, z + nz - away, z + away) & (nz - 1)) + ((row_of >> 3) & 1)
+        target = band * 32 + x * 8 + (row_of & 7)
+        for q in range(4):
+            ref[:, q * 256:(q + 1) * 256] = jnp.where(target == col_of + q * 256, 1.0, 0.0).astype(BF16)
+
+    def prepare_spread(x):
+        place_columns(spread_to.at[x], x)
+        if x == 3:
+            row_of = lax.broadcasted_iota(jnp.int32, (256, 256), 0)
+            col_of = lax.broadcasted_iota(jnp.int32, (256, 256), 1)
+            eye[...] = jnp.where(row_of == col_of, 1.0, 0.0).astype(BF16)
+
     def choose():
         row_of = lax.broadcasted_iota(jnp.int32, (256, 256), 0)
         col_of = lax.broadcasted_iota(jnp.int32, (256, 256), 1)
         ones[...] = jnp.where((row_of >> 5) == (col_of >> 5), 1.0, 0.0).astype(BF16)
-        slot = row_of >> 4
-        away = (slot + 1) >> 1
-        band = 2 * (jnp.where((slot & 1) == 1, z + nz - away, z + away) & (nz - 1)) + ((row_of >> 3) & 1)
-        target = band * 32 + t * 8 + (row_of & 7)
-        for q in range(4):
-            sel[:, q * 256:(q + 1) * 256] = jnp.where(target == col_of + q * 256, 1.0, 0.0).astype(BF16)
+        place_columns(sel, t)
         acc[...] = jnp.zeros_like(acc)
         loads[4].wait()
         mine = lax.dot_general(xa[...], sel[...], (((1,), (1,)), ((), ())), preferred_element_type=F32)
@@ -346,7 +358,7 @@
 
     def backward(hg):
         bs[hg] = lax.dot_general(
-            acc[hg].astype(BF16), sel[...], (((0,), (0,)), ((), ())), preferred_element_type=F32
+            acc[hg].astype(BF16), eye[...], (((0,), (0,)), ((), ())), preferred_element_type=F32
         ).astype(BF16)
         for yy in range(2):
             @pl.when(is_self(hg, yy))
@@ -400,6 +412,7 @@
     def finish_piece(c):
         arrived(c, nz - 1)
         products(c, 3)
+        pl.when(c == nu - 1)(functools.partial(backward, 1))
         results(c)
 
     def step_and_waits(c, s):
@@ -450,10 +463,12 @@
             each(0, nu, functools.partial(step_and_part, s=s, kk=s - steps + 4))
         else:
             each(0, nu, functools.partial(step_and_waits, s=s))
+        if s in (1, 2):
+            prepare_spread(2 * s - 2)
+            prepare_spread(2 * s - 1)
         if s == 3:
             og_pass()
     lax.fori_loop(0, nu + 3, last_steps, 0)
-    backward(1)
     lax.fori_loop(0, nu, sent_last, 0)
     for out in outs:
         out.wait()
@@ -465,7 +480,9 @@
             remote(
                 bs.at[0, pl.ds(0, 32), :], br.at[x], bw_s.at[0], bw_r.at[x], mate
             ).wait_recv()
-    total = br[0].astype(F32) + br[1].astype(F32) + br[2].astype(F32) + br[3].astype(F32)
+    total = jnp.dot(br[0], spread_to[0], preferred_element_type=F32)
+    for x in range(1, 4):
+        total += jnp.dot(br[x], spread_to[x], preferred_element_type=F32)
     bo[...] = total.astype(BF16)
     out_b = pltpu.make_async_copy(bo, o_bwd, out_s.at[3])
     out_b.start()
@@ -523,6 +540,8 @@
             vm((4, 2 * tokens, 80), BF16),
             vm((2, 2 * tokens, hidden // 4), BF16),
             vm((16 * nz, 64 * nz), BF16),
+            vm((4, 16 * nz, 64 * nz), BF16),
+            vm((256, 256), BF16),
             vm((256, 256), BF16),
             vm((nu, 16, 2 * UNIT), BF16),
             vm((nu, 16, 2 * UNIT), BF16),
@@ -537,8 +556,8 @@
             vm((nu, 2 * tokens, UNIT), F32),
             vm((nu, 2 * tokens, UNIT), BF16),
             vm((2, 16 * nz, 2 * tokens), F32),
-            vm((2, 2 * tokens, 64 * nz), BF16),
-            vm((4, tokens, 64 * nz), BF16),
+            vm((2, 2 * tokens, 16 * nz), BF16),
+            vm((4, tokens, 16 * nz), BF16),
             vm((tokens, 64 * nz), BF16),
             dma((5,)),
             dma((nu,)), dma((nu,)), dma((nu,)), dma((nu,)), dma((nu,)), dma((nu,)),

time: 86.3 us -> 82 us (0.950)
  Pallas kernels: 85.5 us -> 81.2 us
    pallas_call x1, Pallas kernels: 82.9 us -> 78.5 us  [local(): pl.pallas_call(functools.partial(kernel, nz, nu), out_shape=results, in_s...]
where the time goes in v4:
time: 82 us; the launch traced here: 81.8 us
  Pallas kernels  81.2 us (99%)
    pallas_call x1, Pallas kernels, local(): pl.pallas_call(functools.partial(kernel, nz, nu), out_shape=results, in_s...  78.5 us
    pallas_call x1, Pallas kernels, local(): pl.pallas_call(hand_over, out_shape=results, in_specs=[any_spec] * 5, out...  2.62 us

profile of v4, /device:TPU:6, one launch (start us, length us, event | category | flops | bytes accessed | tf_op | source)
XLA Modules:
  0.0 81.8 jit_solution(14750872646492130243)
XLA Ops:
  0.6 78.5 %shard_map.101 = (f32[8,14336]{1,0:T(8,128)}, f32[8,14336]{1,0:T(8,128)}, f32[8,14336]{1,0:T(8,128)}, bf16[32,14336]{1,0:T(8,128)(2,1)}, bf16[32,1024]{1,0:T(8,128)(2,1)}) custom-call(f32[8,14336]{1,0:T(8,128)} %bitcast.10, f32[8,14336]{1,0:T(8,128)} %bitcast.11, f32[8,14336]{1,0:T(8,128)} %bitcast.12, bf16[32,14336]{1,0:T(8,128)(2,1)} %bitcast.9, ...), custom_call_target="tpu_custom_call" | custom-call | tf_op jit(solution)/shard_map/pallas_call | solution.py:528
  79.2 2.6 %shard_map.102 = (f32[8,14336]{1,0:T(8,128)}, f32[8,14336]{1,0:T(8,128)}, f32[8,14336]{1,0:T(8,128)}, bf16[32,14336]{1,0:T(8,128)(2,1)}, bf16[32,1024]{1,0:T(8,128)(2,1)}) custom-call(f32[8,14336]{1,0:T(8,128)} %get-tuple-element.15.refs_0_, f32[8,14336]{1,0:T(8,128)} %get-tuple-element.16.refs_1_, f32[8,14336]{1,0:T(8,128)} %get-tuple-element.17.refs_2_, ...), custom_call_target="tpu_custom_call" | custom-call | tf_op jit(solution)/shard_map/pallas_call | solution.py:583
